TPU v7x, 128 devices: a whole 4x4x4 slice. The times are simulated.
128 devices in a mesh: row: 4 (over x_hi, core), col: 4 (over z), depth: 8 (over y, x_lo).
Axes of the slice: x: 4 (x_hi: 2, x_lo: 2; x = x_hi * 2 + x_lo), y: 4, z: 4, core: 2. Of those that a mesh axis runs over, the one named last changes fastest.
Arguments:
- a_blocks: bfloat16 [32, 4, 4, 16, 128, 128], P(None, 'col', 'row', 'depth'), may hold values from -6 to 6
- a_rows: int32 [32, 4, 4, 16], replicated, may hold values from -1 to 31, as said below
- b_blocks: bfloat16 [32, 4, 4, 8, 128, 128], P(None, 'row', 'col', 'depth'), may hold values from -0.15625 to 0.15625
- b_cols: int32 [32, 4, 4, 8], replicated, may hold values from -1 to 15, as said below
- c_pos: int32 [4, 4, 128], P('row', 'col'), may hold values from -1 to 511, as said below
Outputs:
- c_blocks: bfloat16 [4, 4, 128, 128, 128], P('row', 'col', 'depth')
Inputs may be any that keep to these rules, and one draw needn't show every extreme that they name: `a_rows`: for each inner block (g, m) and row group i the live slots come first and hold distinct local block rows, the rest hold -1; each has at least one live slot, and in every draw some (g, m, i) has all 16 slots live. `b_cols`: for each inner block (g, m) and column group h the live slots come first and hold distinct local block columns, the rest hold -1; each has at least one live slot, and in every draw some (g, m, h) has all 8 slots live. `c_pos`: each cell lists distinct positions in its first slots and -1 in the rest; every cell keeps at least one block, and in every draw some cell keeps 128.
All inputs are finite; a program needn't handle non-finite values.
Results may differ from a plain program's by a relative error of at most 0.001.
Values may be sent and summed in bfloat16 or wider, within the bound.
A program may use at most 320 MiB of HBM per device.

v0:
```python
import functools

import jax
import jax.numpy as jnp
from jax import lax
from jax.experimental import pallas as pl
from jax.experimental.pallas import tpu as pltpu
from jax.sharding import PartitionSpec as P

MESH = pl.DeviceIdType.MESH
BS = 128
NBL = 16
MBL = 32
ANY = pl.BlockSpec(memory_space=pl.ANY)
SMEM = pl.BlockSpec(memory_space=pltpu.SMEM)


def place():
    row, z, depth = lax.axis_index("row"), lax.axis_index("col"), lax.axis_index("depth")
    return row // 2, depth % 2, row % 2, depth // 2, z


def device(x_hi, x_lo, core, y, z):
    return (x_hi * 2 + core, z, y * 2 + x_lo)


def remote(src, dst, send, recv, to):
    return pltpu.make_async_remote_copy(
        src_ref=src, dst_ref=dst, send_sem=send, recv_sem=recv, device_id=to, device_id_type=MESH
    )


PIECES = ((0, 0), (0, 1), (1, 0), (1, 1), (3, 0), (3, 1), (2, 0), (2, 1))
LAG = 2


def gather_kernel(
    a_ref, b_ref, c_ref, pa_ref, pb_ref, cs_ref, a_send, a_recv, az_send, b_send, b_recv, bx_send, c_sem
):
    x_hi, x_lo, core, y, z = place()
    x = x_hi * 2 + x_lo
    same = x_lo == core

    def y_at(step):
        return lax.rem(y + step + 4, 4)

    def z_to(step):
        return device(x_hi, x_lo, core, y, lax.rem(z + step + 4, 4))

    def x_to(step):
        to = lax.rem(x + step + 4, 4)
        return device(to // 2, lax.rem(to, 2), core, y, z)

    twin = device(x_hi, x_lo, 1 - core, y, z)

    barrier = pltpu.get_barrier_semaphore()

    def greet(to):
        pl.semaphore_signal(barrier, inc=1, device_id=to, device_id_type=MESH)

    for dy in range(4):
        for other in range(2):
            if (dy, other) == (0, 0):

                @pl.when(jnp.logical_not(same))
                def _():
                    greet(device(x_hi, x_lo, x_lo, y, z))

            else:
                lo = x_lo if other == 0 else 1 - x_lo
                greet(device(x_hi, lo, x_lo, y_at(-dy), z))
            if (dy, other) != (0, 0):
                greet(device(x_hi, x_lo, core if other == 0 else 1 - core, y_at(-dy), z))
    for step in (1, -1):
        greet(z_to(step))
        greet(x_to(step))
    apart = jnp.where(same, 0, 1)
    pl.semaphore_wait(barrier, 18 + apart)

    d_here = y * 2 + x_lo
    m_here = x_hi * 2 + core
    a_out, b_out = [], []
    for j, (dy, other) in enumerate(PIECES):
        to_y = y_at(dy)
        to_core = core if other == 0 else 1 - core
        layer = to_y * 2 + to_core
        src = a_ref.at[pl.ds(layer * 4, 4)]
        dst = pa_ref.at[z, d_here]
        sem = a_recv.at[0, dy * 2 + apart]
        copy = remote(src, dst, a_send.at[j], sem, device(x_hi, core, to_core, to_y, z))
        if (dy, other) == (0, 0):
            stay = pltpu.make_async_copy(src, dst, sem)

            @pl.when(same)
            def _():
                stay.start()

            @pl.when(jnp.logical_not(same))
            def _():
                copy.start()

            first_out = copy
        else:
            copy.start()
            a_out.append(copy)
    copy = remote(c_ref, cs_ref, c_sem.at[0], c_sem.at[1], twin)
    copy.start()
    c_out = copy
    for j, (dy, other) in enumerate(PIECES):
        to_y = y_at(dy)
        to_core = core if other == 0 else 1 - core
        layer = to_y * 2 + to_core
        src = b_ref.at[pl.ds(layer * 4, 4)]
        dst = pb_ref.at[m_here, d_here]
        sem = b_recv.at[0, dy * 2 + other]
        if (dy, other) == (0, 0):
            pltpu.make_async_copy(src, dst, sem).start()
        else:
            copy = remote(src, dst, b_send.at[j], sem, device(x_hi, x_lo, to_core, to_y, z))
            copy.start()
            b_out.append(copy)

    def a_slot(back, dy, other):
        lo = x_lo if other == 0 else 1 - x_lo
        return pa_ref.at[lax.rem(z - back + 4, 4), y_at(-dy) * 2 + lo]

    def b_slot(back, dy, other):
        from_x = lax.rem(x - back + 4, 4)
        from_core = core if other == 0 else 1 - core
        return pb_ref.at[(from_x // 2) * 2 + from_core, y_at(-dy) * 2 + lax.rem(from_x, 2)]

    def turn(slot, recv, send, to, out, j):
        dy, other = PIECES[j]
        n = dy * 2 + other
        here = slot(0, dy, other)
        remote(here, here, send.at[0, n], recv.at[0, n], to(1)).wait_recv()
        for way, step in ((0, 1), (1, -1)):
            copy = remote(here, here, send.at[way, n], recv.at[1 if step == 1 else 3, n], to(step))
            copy.start()
            out.append(copy)

    def pass_on(slot, recv, send, to, out, j):
        dy, other = PIECES[j]
        n = dy * 2 + other
        back, step = (1, 1) if j % 2 == 0 else (3, -1)
        piece = slot(back, dy, other)
        remote(piece, piece, send.at[2, n], recv.at[back, n], to(step)).wait_recv()
        copy = remote(piece, piece, send.at[2, n], recv.at[2, n], to(step))
        copy.start()
        out.append(copy)

    a_args = (a_slot, a_recv, az_send, z_to, a_out)
    b_args = (b_slot, b_recv, bx_send, x_to, b_out)
    for j in range(8 + LAG):
        if j < 8:
            turn(*a_args, j)
            turn(*b_args, j)
        if j >= LAG:
            pass_on(*a_args, j - LAG)
            pass_on(*b_args, j - LAG)
    for j, (dy, other) in enumerate(PIECES):
        n = dy * 2 + other
        for back in (3 if j % 2 == 0 else 1, 2):
            piece = a_slot(back, dy, other)
            remote(piece, piece, az_send.at[0, n], a_recv.at[back, n], z_to(1)).wait_recv()
            piece = b_slot(back, dy, other)
            remote(piece, piece, bx_send.at[0, n], b_recv.at[back, n], x_to(1)).wait_recv()
    for copy in a_out + b_out:
        copy.wait_send()
    c_out.wait()

    @pl.when(jnp.logical_not(same))
    def _():
        first_out.wait_send()


def gather_panels(a_local, b_local, c_pos):
    dma = pltpu.SemaphoreType.DMA
    return pl.pallas_call(
        gather_kernel,
        out_shape=(
            jax.ShapeDtypeStruct((4, 8, 4, 2, BS, BS), jnp.bfloat16),
            jax.ShapeDtypeStruct((4, 8, 4, BS, BS), jnp.bfloat16),
            jax.ShapeDtypeStruct(c_pos.shape, jnp.int32),
        ),
        in_specs=[ANY] * 3,
        out_specs=(ANY,) * 3,
        scratch_shapes=[
            dma((8,)), dma((4, 8)), dma((3, 8)), dma((8,)), dma((4, 8)), dma((3, 8)), dma((2,)),
        ],
        compiler_params=pltpu.CompilerParams(collective_id=0, has_side_effects=True),
        name="gather_panels",
    )(a_local, b_local, c_pos)


BATCH = 4
TABLE = (MBL + 1) * (NBL + 1) + 15


def product_kernel(
    rows_ref, cols_ref, mine_ref, twin_ref, pa_ref, pb_ref, out_ref, a_buf, b_buf, total, table, jobs, sem
):
    _, x_lo, core, _, _ = place()
    loads = [
        pltpu.make_async_copy(pa_ref, a_buf, sem.at[0]),
        pltpu.make_async_copy(pb_ref, b_buf, sem.at[1]),
    ]
    for load in loads:
        load.start()

    def clear(at, _):
        table[at] = -1
        return 0

    lax.fori_loop(0, TABLE, clear, 0, unroll=16)

    def enter(slot, _):
        spot = jnp.where(x_lo == core, mine_ref[0, 0, slot], twin_ref[0, 0, slot])
        at = (spot // NBL + 1) * (NBL + 1) + spot % NBL + 1
        table[jnp.where(spot >= 0, at, 0)] = jnp.where(spot >= 0, slot, -1)
        return 0

    lax.fori_loop(0, BS, enter, 0, unroll=8)

    def inner(k, count):
        g, m = k // 4, k % 4
        cols = [cols_ref[k, v] + 1 for v in range(8)]

        def one_row(u, count):
            at = (rows_ref[k, u] + 1) * (NBL + 1)
            a_at = ((m * 8 + u // 2) * 4 + g) * 2 + u % 2
            for v in range(8):
                slot = table[at + cols[v]]
                jobs[count] = (a_at * 128 + ((m * 8 + v) * 4 + g)) * 256 + slot
                count = count + jnp.where(slot >= 0, 1, 0)
            return count

        return lax.fori_loop(0, rows_ref[k, 16], one_row, count)

    count = lax.fori_loop(0, 16, inner, 0)
    for extra in range(BATCH):
        jobs[count + extra] = BS

    def blank(slot, _):
        total[slot] = jnp.zeros((BS, BS), jnp.float32)
        return 0

    lax.fori_loop(0, BS + 1, blank, 0)
    for load in loads:
        load.wait()

    def batch(at, _):
        slots, terms = [], []
        for n in range(BATCH):
            job = jobs[at * BATCH + n]
            slots.append(job % 256)
            terms.append(
                jnp.dot(
                    a_buf[job // 32768], b_buf[(job // 256) % 128], preferred_element_type=jnp.float32
                )
            )
        for slot, term in zip(slots, terms):
            total[slot] += term
        return 0

    lax.fori_loop(0, (count + BATCH - 1) // BATCH, batch, 0)
    store = pltpu.make_async_copy(total.at[pl.ds(0, BS)], out_ref, sem.at[0])
    store.start()
    store.wait()


def partial_sums(rows, cols, mine, twin, panel_a, panel_b):
    return pl.pallas_call(
        product_kernel,
        out_shape=jax.ShapeDtypeStruct((BS, BS, BS), jnp.float32),
        in_specs=[SMEM] * 4 + [ANY] * 2,
        out_specs=ANY,
        scratch_shapes=[
            pltpu.VMEM(panel_a.shape, jnp.bfloat16),
            pltpu.VMEM(panel_b.shape, jnp.bfloat16),
            pltpu.VMEM((BS + 1, BS, BS), jnp.float32),
            pltpu.SMEM((TABLE,), jnp.int32),
            pltpu.SMEM((16 * 128 + BATCH,), jnp.int32),
            pltpu.SemaphoreType.DMA((2,)),
        ],
        compiler_params=pltpu.CompilerParams(vmem_limit_bytes=40 * 2**20),
        name="partial_sums",
    )(rows, cols, mine, twin, panel_a, panel_b)


def reduce_kernel(
    part_ref, out_ref, own, other, via, got, done, load_sem, twin_sem, via_sem, got_sem, out_sem
):
    x_hi, x_lo, core, y, z = place()
    same = x_lo == core

    def y_at(step):
        return lax.rem(y + step + 4, 4)

    def y_to(step):
        return device(x_hi, x_lo, core, y_at(step), z)

    twin = device(x_hi, x_lo, 1 - core, y, z)
    owner = device(x_hi, core, x_lo, y, z)

    barrier = pltpu.get_barrier_semaphore()

    def greet(to):
        pl.semaphore_signal(barrier, inc=1, device_id=to, device_id_type=MESH)

    greet(twin)
    greet(y_to(1))
    greet(y_to(-1))

    @pl.when(jnp.logical_not(same))
    def _():
        greet(owner)

    pl.semaphore_wait(barrier, 3 + jnp.where(same, 0, 1))

    order = (2, 1, 3, 0)
    loads, twins, sent = {}, {}, []
    for r in order:
        loads[r] = pltpu.make_async_copy(part_ref.at[y_at(r), core], own.at[r], load_sem.at[r])
        loads[r].start()
        twins[r] = remote(
            part_ref.at[y_at(r), 1 - core], other.at[r], twin_sem.at[0, r], twin_sem.at[1, r], twin
        )
        twins[r].start()

    def add(into, r, first, count, term):
        def one(n, _):
            into[r, first + n] += term[n]
            return 0

        lax.fori_loop(0, count, one, 0)

    def meet(r):
        loads[r].wait()
        twins[r].wait_recv()
        add(own, r, 0, 16, other.at[r])

    def send(src, dst, sems, to):
        copy = remote(src, dst, sems[0], sems[1], to)
        copy.start()
        sent.append(copy)
        return copy

    def pair(sems, n):
        return sems.at[0, n], sems.at[1, n]

    meet(2)
    via_up = send(own.at[2, pl.ds(0, 8)], via.at[0], pair(via_sem, 0), y_to(1))
    via_down = send(own.at[2, pl.ds(8, 8)], via.at[1], pair(via_sem, 1), y_to(-1))
    meet(1)
    up_late = send(own.at[1, pl.ds(8, 8)], got.at[0, pl.ds(8, 8)], pair(got_sem, 0), y_to(1))
    meet(3)
    down_early = send(own.at[3, pl.ds(0, 8)], got.at[1, pl.ds(0, 8)], pair(got_sem, 1), y_to(-1))
    via_up.wait_recv()
    add(own, 1, 0, 8, via.at[0])
    up_early = send(own.at[1, pl.ds(0, 8)], got.at[0, pl.ds(0, 8)], pair(got_sem, 2), y_to(1))
    via_down.wait_recv()
    add(own, 3, 8, 8, via.at[1])
    down_late = send(own.at[3, pl.ds(8, 8)], got.at[1, pl.ds(8, 8)], pair(got_sem, 3), y_to(-1))
    meet(0)
    up_late.wait_recv()
    add(own, 0, 8, 8, got.at[0, pl.ds(8, 8)])
    down_early.wait_recv()
    add(own, 0, 0, 8, got.at[1, pl.ds(0, 8)])

    def finish(half, from_way):
        first = half * 8

        def one(n, _):
            done[first + n] = (own[0, first + n] + got[from_way, first + n]).astype(jnp.bfloat16)
            return 0

        lax.fori_loop(0, 8, one, 0)
        span = pl.ds(first, 8)

        @pl.when(same)
        def _():
            pltpu.make_async_copy(done.at[span], out_ref.at[span], out_sem.at[1, half]).start()

        @pl.when(jnp.logical_not(same))
        def _():
            remote(done.at[span], out_ref.at[span], out_sem.at[0, half], out_sem.at[1, half], owner).start()

    up_early.wait_recv()
    finish(0, 0)
    down_late.wait_recv()
    finish(1, 1)
    for half in range(2):
        span = pl.ds(half * 8, 8)
        copy = remote(done.at[span], out_ref.at[span], out_sem.at[0, half], out_sem.at[1, half], owner)
        copy.wait_recv()

        @pl.when(jnp.logical_not(same))
        def _():
            copy.wait_send()

    for copy in sent:
        copy.wait_send()
    for r in order:
        twins[r].wait_send()


def reduce_sums(part):
    dma = pltpu.SemaphoreType.DMA
    f32 = jnp.float32
    return pl.pallas_call(
        reduce_kernel,
        out_shape=jax.ShapeDtypeStruct((16, BS, BS), jnp.bfloat16),
        in_specs=[ANY],
        out_specs=ANY,
        scratch_shapes=[
            pltpu.VMEM((4, 16, BS, BS), f32),
            pltpu.VMEM((4, 16, BS, BS), f32),
            pltpu.VMEM((2, 8, BS, BS), f32),
            pltpu.VMEM((2, 16, BS, BS), f32),
            pltpu.VMEM((16, BS, BS), jnp.bfloat16),
            dma((4,)), dma((2, 4)), dma((2, 2)), dma((2, 4)), dma((2, 2)),
        ],
        compiler_params=pltpu.CompilerParams(
            collective_id=1, has_side_effects=True, vmem_limit_bytes=40 * 2**20
        ),
        name="reduce_sums",
    )(part)


def per_device(a_blocks, a_rows, b_blocks, b_cols, c_pos):
    x_hi, x_lo, core, y, z = place()
    layer = y * 2 + core
    rows = lax.dynamic_slice(a_rows, (layer * 4, 0, x_hi * 2 + x_lo, 0), (4, 4, 1, 16)).reshape(16, 16)
    rows = jnp.concatenate([rows, jnp.sum(rows >= 0, axis=1, keepdims=True, dtype=jnp.int32)], axis=1)
    cols = lax.dynamic_slice(b_cols, (layer * 4, 0, z, 0), (4, 4, 1, 8)).reshape(16, 8)
    panel_a, panel_b, twin_pos = gather_panels(a_blocks[:, 0, 0], b_blocks[:, 0, 0, 0], c_pos)
    part = partial_sums(
        rows, cols, c_pos, twin_pos, panel_a.reshape(256, BS, BS), panel_b.reshape(128, BS, BS)
    )
    return reduce_sums(part.reshape(4, 2, 16, BS, BS))[None, None]


def solution(mesh):
    placed = (
        P(None, "col", "row", "depth", None, None),
        P(),
        P(None, "row", "col", "depth", None, None),
        P(),
        P("row", "col", None),
    )
    return jax.shard_map(
        per_device,
        mesh=mesh,
        in_specs=placed,
        out_specs=P("row", "col", "depth", None, None),
        check_vma=False,
    )
```

profile of v0, /device:TPU:57, one launch (start us, length us, event | category | flops | bytes accessed | tf_op | source)
XLA Modules:
  0.0 162.7 jit_solution(6493303556730423796)
XLA Ops:
  0.0 0.0 copy-start
  0.0 0.8 copy-done
  0.8 0.1 constant_dynamic-slice_fusion
  0.9 0.1 copy.12
  1.0 0.8 convert_reduce_fusion
  1.9 0.1 copy.10
  2.0 0.1 broadcast_in_dim.8
  2.0 0.1 copy.9
  2.1 0.1 pad_add_fusion.rows_ref
  2.2 84.7 %gather_panels.1 = (bf16[4,8,4,2,128,128]{5,4,3,2,1,0:T(8,128)(2,1)}, bf16[4,8,4,128,128]{4,3,2,1,0:T(8,128)(2,1)}, s32[1,1,128]{2,1,0:T(1,128)}) custom-call(bf16[32,2,128,128]{3,2,1,0:T(8,128)(2,1)} %bitcast.13, bf16[32,128,128]{2,1,0:T(8,128)(2,1)} %bitcast.14, s32[1,1,128]{2,1,0:T(1,128)} %mine_ref.1), custom_call_target="tpu_custom_call" | custom-call | tf_op jit(solution)/shard_map/gather_panels/pallas_call | solution.py:179
  86.9 0.0 copy-start.1
  86.9 2.2 %copy-done.1 = bf16[4,8,4,128,128]{4,3,2,1,0:T(8,128)(2,1)S(1)} copy-done((bf16[4,8,4,128,128]{4,3,2,1,0:T(8,128)(2,1)S(1)}, bf16[4,8,4,128,128]{4,3,2,1,0:T(8,128)(2,1)}, u32[]{:S(2)}) %copy-start.1) | copy-done | bytes 4194328
  89.1 0.0 copy-start.2
  89.1 0.7 copy-done.2
  89.7 0.0 copy-start.3
  89.7 0.6 copy-done.3
  90.4 18.2 %partial_sums.1 = f32[128,128,128]{2,1,0:T(8,128)S(1)} custom-call(s32[16,17]{1,0:T(8,128)S(1)} %pad_add_fusion.rows_ref, s32[16,8]{1,0:T(8,128)S(1)} %bitcast.11, s32[1,1,128]{2,1,0:T(1,128)S(1)} %copy-done.2, s32[1,1,128]{2,1,0:T(1,128)S(1)} %copy-done.3, bf16[256,128,128]{2,1,0:T(8,128)(2,1)} %bitcast.12, bf16[128,128,128]{2,1,0:T(8,128)(2,1)S(1)} %bitcast.9), custom_call_target="tpu_custom_call" | custom-call | tf_op jit(solution)/shard_map/partial_sums/pallas_call | solution.py:273
  108.6 53.3 %reduce_sums.1 = bf16[16,128,128]{2,1,0:T(8,128)(2,1)S(1)} custom-call(f32[4,2,16,128,128]{4,3,2,1,0:T(8,128)S(1)} %bitcast.8), custom_call_target="tpu_custom_call" | custom-call | tf_op jit(solution)/shard_map/reduce_sums/pallas_call | solution.py:411
  161.9 0.8 copy.14
Async XLA Ops:
  0.0 0.8 copy-start
  86.9 2.2 %copy-start.1 = (bf16[4,8,4,128,128]{4,3,2,1,0:T(8,128)(2,1)S(1)}, bf16[4,8,4,128,128]{4,3,2,1,0:T(8,128)(2,1)}, u32[]{:S(2)}) copy-start(bf16[4,8,4,128,128]{4,3,2,1,0:T(8,128)(2,1)} %get-tuple-element.10) | copy-start | bytes 12582916
  89.1 0.7 copy-start.2
  89.7 0.6 copy-start.3
where the time goes:
time: 163 us
  Pallas kernels  156 us (96%)
  local copies, waits for them, and re-layouts  5.55 us (3%)
    pallas_call x1, Pallas kernels, gather_panels(): pl.pallas_call(gather_kernel, out_shape=(jax.ShapeDtypeStruct((4, 8, 4, 2...  84.7 us
    pallas_call x1, Pallas kernels, reduce_sums(): pl.pallas_call(reduce_kernel, out_shape=jax.ShapeDtypeStruct((16, BS, BS)...  53.3 us
    pallas_call x1, Pallas kernels, partial_sums(): pl.pallas_call(product_kernel, out_shape=jax.ShapeDtypeStruct((BS, BS, BS...  18.2 us
    unnamed x9, local copies, waits for them, and re-layouts  5.11 us

commit v1 on v0

--- a/solution.py
+++ b/solution.py
@@ -10,9 +10,7 @@
 MESH = pl.DeviceIdType.MESH
 BS = 128
 NBL = 16
-MBL = 32
 ANY = pl.BlockSpec(memory_space=pl.ANY)
-SMEM = pl.BlockSpec(memory_space=pltpu.SMEM)
 
 
 def place():
@@ -31,7 +29,11 @@
 
 
 PIECES = ((0, 0), (0, 1), (1, 0), (1, 1), (3, 0), (3, 1), (2, 0), (2, 1))
-LAG = 2
+SCHEDULE = (
+    "ta0", "tb0", "ta1", "tb1", "ta2", "pa0", "ta3", "pa1", "ta4", "pa2", "ta5", "pa3", "ta6",
+    "pa4", "ta7", "tb2", "pb0", "tb3", "pb1", "tb4", "pb2", "tb5", "pb3", "pa5", "tb6", "pb4",
+    "tb7", "pa6", "pb5", "pa7", "pb6", "pb7",
+)
 
 
 def gather_kernel(
@@ -151,13 +153,9 @@
 
     a_args = (a_slot, a_recv, az_send, z_to, a_out)
     b_args = (b_slot, b_recv, bx_send, x_to, b_out)
-    for j in range(8 + LAG):
-        if j < 8:
-            turn(*a_args, j)
-            turn(*b_args, j)
-        if j >= LAG:
-            pass_on(*a_args, j - LAG)
-            pass_on(*b_args, j - LAG)
+    for entry in SCHEDULE:
+        step = turn if entry[0] == "t" else pass_on
+        step(*(a_args if entry[1] == "a" else b_args), int(entry[2]))
     for j, (dy, other) in enumerate(PIECES):
         n = dy * 2 + other
         for back in (3 if j % 2 == 0 else 1, 2):
@@ -188,108 +186,162 @@
         scratch_shapes=[
             dma((8,)), dma((4, 8)), dma((3, 8)), dma((8,)), dma((4, 8)), dma((3, 8)), dma((2,)),
         ],
-        compiler_params=pltpu.CompilerParams(collective_id=0, has_side_effects=True),
+        compiler_params=pltpu.CompilerParams(
+            collective_id=0, has_side_effects=True, vmem_limit_bytes=60 * 2**20
+        ),
         name="gather_panels",
     )(a_local, b_local, c_pos)
 
 
-BATCH = 4
-TABLE = (MBL + 1) * (NBL + 1) + 15
+EXTRA = 4
+NONE = 256 * 128
 
 
 def product_kernel(
-    rows_ref, cols_ref, mine_ref, twin_ref, pa_ref, pb_ref, out_ref, a_buf, b_buf, total, table, jobs, sem
+    rows_hbm, cols_hbm, mine_ref, twin_ref, pa_ref, pb_ref, out_ref,
+    a_buf, b_buf, total, rows, cols, spots, jobs_v, jobs, extras, ends, sem,
 ):
     _, x_lo, core, _, _ = place()
+    small = [
+        pltpu.make_async_copy(rows_hbm, rows, sem.at[0]),
+        pltpu.make_async_copy(cols_hbm, cols, sem.at[1]),
+        pltpu.make_async_copy(mine_ref, spots.at[0], sem.at[2]),
+        pltpu.make_async_copy(twin_ref, spots.at[1], sem.at[3]),
+    ]
     loads = [
-        pltpu.make_async_copy(pa_ref, a_buf, sem.at[0]),
-        pltpu.make_async_copy(pb_ref, b_buf, sem.at[1]),
+        pltpu.make_async_copy(pa_ref, a_buf.at[pl.ds(0, 256)], sem.at[4]),
+        pltpu.make_async_copy(pb_ref, b_buf, sem.at[5]),
     ]
-    for load in loads:
-        load.start()
-
-    def clear(at, _):
-        table[at] = -1
-        return 0
-
-    lax.fori_loop(0, TABLE, clear, 0, unroll=16)
-
-    def enter(slot, _):
-        spot = jnp.where(x_lo == core, mine_ref[0, 0, slot], twin_ref[0, 0, slot])
-        at = (spot // NBL + 1) * (NBL + 1) + spot % NBL + 1
-        table[jnp.where(spot >= 0, at, 0)] = jnp.where(spot >= 0, slot, -1)
-        return 0
-
-    lax.fori_loop(0, BS, enter, 0, unroll=8)
-
-    def inner(k, count):
-        g, m = k // 4, k % 4
-        cols = [cols_ref[k, v] + 1 for v in range(8)]
-
-        def one_row(u, count):
-            at = (rows_ref[k, u] + 1) * (NBL + 1)
-            a_at = ((m * 8 + u // 2) * 4 + g) * 2 + u % 2
-            for v in range(8):
-                slot = table[at + cols[v]]
-                jobs[count] = (a_at * 128 + ((m * 8 + v) * 4 + g)) * 256 + slot
-                count = count + jnp.where(slot >= 0, 1, 0)
-            return count
-
-        return lax.fori_loop(0, rows_ref[k, 16], one_row, count)
-
-    count = lax.fori_loop(0, 16, inner, 0)
-    for extra in range(BATCH):
-        jobs[count + extra] = BS
-
-    def blank(slot, _):
-        total[slot] = jnp.zeros((BS, BS), jnp.float32)
-        return 0
-
-    lax.fori_loop(0, BS + 1, blank, 0)
+    for copy in small + loads:
+        copy.start()
+    a_buf[256] = jnp.zeros((BS, BS), jnp.bfloat16)
+    for copy in small:
+        copy.wait()
+
+    spot = jnp.where(x_lo == core, spots[0, 0], spots[1, 0])
+    kept_row = jnp.where(spot >= 0, spot // NBL, -2)
+    kept_col = jnp.where(spot >= 0, spot % NBL, -2)
+    k = lax.broadcasted_iota(jnp.int32, (16, BS), 0)
+    a_base = (k % 4) * 64 + (k // 4) * 2
+    b_base = (k % 4) * 32 + k // 4
+    a_at = jnp.full((16, BS), -1, jnp.int32)
+    b_at = jnp.full((16, BS), -1, jnp.int32)
+    row_values, col_values = rows[...], cols[...]
+    for u in range(16):
+        a_at = jnp.where(row_values[:, u : u + 1] == kept_row, a_base + (u // 2 * 8 + u % 2), a_at)
+    for v in range(8):
+        b_at = jnp.where(col_values[:, v : v + 1] == kept_col, b_base + v * 4, b_at)
+    code = jnp.where((a_at >= 0) & (b_at >= 0), a_at * 128 + b_at, NONE)
+
+    found = [jnp.full((1, BS), NONE, jnp.int32) for _ in range(16)]
+    count = jnp.zeros((1, BS), jnp.int32)
+    for k in range(16):
+        one = code[k : k + 1]
+        live = one < NONE
+        for j in range(k + 1):
+            found[j] = jnp.where(live & (count == j), one, found[j])
+        count = count + live.astype(jnp.int32)
+    for j in range(16):
+        jobs_v[j : j + 1] = found[j]
+    jobs_v[16:17] = count
+    jobs_v[18:20] = jnp.full((2, BS), NONE, jnp.int32)
+    copy = pltpu.make_async_copy(jobs_v, jobs, sem.at[0])
+    copy.start()
+    copy.wait()
+
+    def list_quarter(q, filled):
+        def list_pairs(pair, filled):
+            def one_slot(n, filled):
+                slot = q * 32 + n
+                extras[filled] = slot * 32 + pair * 2
+                return filled + jnp.where(jobs[16, slot] > pair * 2, 1, 0)
+
+            return lax.fori_loop(0, 32, one_slot, filled, unroll=8)
+
+        def most(n, value):
+            return jnp.maximum(value, jobs[16, q * 32 + n])
+
+        pairs = (lax.fori_loop(0, 32, most, 0, unroll=8) + 1) // 2
+        filled = lax.fori_loop(1, pairs, list_pairs, filled)
+        for n in range(EXTRA - 1):
+            extras[filled + n] = q * 1024 + 18
+        filled = (filled + EXTRA - 1) // EXTRA * EXTRA
+        ends[q + 1] = filled
+        return filled
+
+    ends[0] = 0
+    lax.fori_loop(0, 4, list_quarter, 0)
     for load in loads:
         load.wait()
 
-    def batch(at, _):
-        slots, terms = [], []
-        for n in range(BATCH):
-            job = jobs[at * BATCH + n]
-            slots.append(job % 256)
-            terms.append(
-                jnp.dot(
-                    a_buf[job // 32768], b_buf[(job // 256) % 128], preferred_element_type=jnp.float32
-                )
-            )
-        for slot, term in zip(slots, terms):
-            total[slot] += term
+    def pair_product(first, second):
+        left = jnp.concatenate([a_buf[first // 128], a_buf[second // 128]], axis=1)
+        right = jnp.concatenate([b_buf[first % 128], b_buf[second % 128]], axis=0)
+        return jnp.dot(left, right, preferred_element_type=jnp.float32)
+
+    def quarter(q, _):
+        def some_slots(n, _):
+            for s in range(8):
+                slot = q * 32 + n * 8 + s
+                total[slot] = pair_product(jobs[0, slot], jobs[1, slot])
+            return 0
+
+        lax.fori_loop(0, 4, some_slots, 0)
+
+        def some_extras(n, _):
+            entries = [extras[n * EXTRA + e] for e in range(EXTRA)]
+            terms = [
+                pair_product(jobs[entry % 32, entry // 32], jobs[entry % 32 + 1, entry // 32])
+                for entry in entries
+            ]
+            for entry, term in zip(entries, terms):
+                total[entry // 32] += term
+            return 0
+
+        lax.fori_loop(ends[q] // EXTRA, ends[q + 1] // EXTRA, some_extras, 0)
+        span = pl.ds(q * 32, 32)
+        pltpu.make_async_copy(total.at[span], out_ref.at[span], sem.at[q]).start()
         return 0
 
-    lax.fori_loop(0, (count + BATCH - 1) // BATCH, batch, 0)
-    store = pltpu.make_async_copy(total.at[pl.ds(0, BS)], out_ref, sem.at[0])
-    store.start()
-    store.wait()
+    lax.fori_loop(0, 4, quarter, 0)
+    for q in range(4):
+        span = pl.ds(q * 32, 32)
+        pltpu.make_async_copy(total.at[span], out_ref.at[span], sem.at[q]).wait()
 
 
 def partial_sums(rows, cols, mine, twin, panel_a, panel_b):
+    i32 = jnp.int32
     return pl.pallas_call(
         product_kernel,
         out_shape=jax.ShapeDtypeStruct((BS, BS, BS), jnp.float32),
-        in_specs=[SMEM] * 4 + [ANY] * 2,
+        in_specs=[ANY] * 6,
         out_specs=ANY,
         scratch_shapes=[
-            pltpu.VMEM(panel_a.shape, jnp.bfloat16),
-            pltpu.VMEM(panel_b.shape, jnp.bfloat16),
-            pltpu.VMEM((BS + 1, BS, BS), jnp.float32),
-            pltpu.SMEM((TABLE,), jnp.int32),
-            pltpu.SMEM((16 * 128 + BATCH,), jnp.int32),
-            pltpu.SemaphoreType.DMA((2,)),
+            pltpu.VMEM((257, BS, BS), jnp.bfloat16),
+            pltpu.VMEM((128, BS, BS), jnp.bfloat16),
+            pltpu.VMEM((BS, BS, BS), jnp.float32),
+            pltpu.VMEM(rows.shape, i32),
+            pltpu.VMEM(cols.shape, i32),
+            pltpu.VMEM((2,) + mine.shape, i32),
+            pltpu.VMEM((24, BS), i32),
+            pltpu.SMEM((24, BS), i32),
+            pltpu.SMEM((1024,), i32),
+            pltpu.SMEM((8,), i32),
+            pltpu.SemaphoreType.DMA((6,)),
         ],
-        compiler_params=pltpu.CompilerParams(vmem_limit_bytes=40 * 2**20),
+        compiler_params=pltpu.CompilerParams(vmem_limit_bytes=60 * 2**20),
         name="partial_sums",
     )(rows, cols, mine, twin, panel_a, panel_b)
 
 
+TOP = 32767.0
+TINY = 2e-34
+HALF = 8
+
+
 def reduce_kernel(
-    part_ref, out_ref, own, other, via, got, done, load_sem, twin_sem, via_sem, got_sem, out_sem
+    part_ref, out_ref, own, other, done_ref, q_out, s_out, q_in, s_in,
+    load_sem, twin_sem, q_send, q_recv, s_send, s_recv, out_sem,
 ):
     x_hi, x_lo, core, y, z = place()
     same = x_lo == core
@@ -316,83 +368,90 @@
     def _():
         greet(owner)
 
-    pl.semaphore_wait(barrier, 3 + jnp.where(same, 0, 1))
-
+    loads, twins, sent = {}, {}, []
     order = (2, 1, 3, 0)
-    loads, twins, sent = {}, {}, []
     for r in order:
         loads[r] = pltpu.make_async_copy(part_ref.at[y_at(r), core], own.at[r], load_sem.at[r])
         loads[r].start()
+    pl.semaphore_wait(barrier, 3 + jnp.where(same, 0, 1))
+    for r in order:
         twins[r] = remote(
             part_ref.at[y_at(r), 1 - core], other.at[r], twin_sem.at[0, r], twin_sem.at[1, r], twin
         )
         twins[r].start()
 
-    def add(into, r, first, count, term):
-        def one(n, _):
-            into[r, first + n] += term[n]
-            return 0
-
-        lax.fori_loop(0, count, one, 0)
-
     def meet(r):
         loads[r].wait()
         twins[r].wait_recv()
-        add(own, r, 0, 16, other.at[r])
-
-    def send(src, dst, sems, to):
-        copy = remote(src, dst, sems[0], sems[1], to)
-        copy.start()
-        sent.append(copy)
-        return copy
-
-    def pair(sems, n):
-        return sems.at[0, n], sems.at[1, n]
+
+    def arrived(i):
+        remote(q_in.at[i], q_in.at[i], q_send.at[i], q_recv.at[i], twin).wait_recv()
+        remote(s_in.at[i], s_in.at[i], s_send.at[i], s_recv.at[i], twin).wait_recv()
+
+    def chip_sum(r, slot):
+        return own[r, slot] + other[r, slot]
+
+    def value(i, n):
+        return q_in[i, n].astype(jnp.float32) * s_in[i, pl.ds(n, 1)]
+
+    def pass_on(i, step, r, first, plus=None):
+        def one(n, _):
+            sums = chip_sum(r, first + n)
+            if plus is not None:
+                sums = sums + value(plus, n)
+            top = jnp.maximum(jnp.max(jnp.abs(sums), axis=0, keepdims=True), TINY)
+            q_out[i, n] = jnp.round(sums * (TOP / top)).astype(jnp.int32).astype(jnp.int16)
+            s_out[i, pl.ds(n, 1)] = top * (1 / TOP)
+            return 0
+
+        lax.fori_loop(0, HALF, one, 0)
+        for src, dst, send, recv in ((q_out, q_in, q_send, q_recv), (s_out, s_in, s_send, s_recv)):
+            copy = remote(src.at[i], dst.at[i], send.at[i], recv.at[i], y_to(step))
+            copy.start()
+            sent.append(copy)
 
     meet(2)
-    via_up = send(own.at[2, pl.ds(0, 8)], via.at[0], pair(via_sem, 0), y_to(1))
-    via_down = send(own.at[2, pl.ds(8, 8)], via.at[1], pair(via_sem, 1), y_to(-1))
+    pass_on(0, 1, 2, 0)
+    pass_on(1, -1, 2, HALF)
     meet(1)
-    up_late = send(own.at[1, pl.ds(8, 8)], got.at[0, pl.ds(8, 8)], pair(got_sem, 0), y_to(1))
+    pass_on(2, 1, 1, HALF)
     meet(3)
-    down_early = send(own.at[3, pl.ds(0, 8)], got.at[1, pl.ds(0, 8)], pair(got_sem, 1), y_to(-1))
-    via_up.wait_recv()
-    add(own, 1, 0, 8, via.at[0])
-    up_early = send(own.at[1, pl.ds(0, 8)], got.at[0, pl.ds(0, 8)], pair(got_sem, 2), y_to(1))
-    via_down.wait_recv()
-    add(own, 3, 8, 8, via.at[1])
-    down_late = send(own.at[3, pl.ds(8, 8)], got.at[1, pl.ds(8, 8)], pair(got_sem, 3), y_to(-1))
+    pass_on(3, -1, 3, 0)
+    arrived(0)
+    pass_on(4, 1, 1, 0, plus=0)
+    arrived(1)
+    pass_on(5, -1, 3, HALF, plus=1)
     meet(0)
-    up_late.wait_recv()
-    add(own, 0, 8, 8, got.at[0, pl.ds(8, 8)])
-    down_early.wait_recv()
-    add(own, 0, 0, 8, got.at[1, pl.ds(0, 8)])
-
-    def finish(half, from_way):
-        first = half * 8
-
+
+    def finish(half, first, second):
         def one(n, _):
-            done[first + n] = (own[0, first + n] + got[from_way, first + n]).astype(jnp.bfloat16)
+            slot = half * HALF + n
+            sums = chip_sum(0, slot) + value(first, n) + value(second, n)
+            done_ref[slot] = sums.astype(jnp.bfloat16)
             return 0
 
-        lax.fori_loop(0, 8, one, 0)
-        span = pl.ds(first, 8)
+        lax.fori_loop(0, HALF, one, 0)
+        span = pl.ds(half * HALF, HALF)
 
         @pl.when(same)
         def _():
-            pltpu.make_async_copy(done.at[span], out_ref.at[span], out_sem.at[1, half]).start()
+            pltpu.make_async_copy(done_ref.at[span], out_ref.at[span], out_sem.at[1, half]).start()
 
         @pl.when(jnp.logical_not(same))
         def _():
-            remote(done.at[span], out_ref.at[span], out_sem.at[0, half], out_sem.at[1, half], owner).start()
-
-    up_early.wait_recv()
-    finish(0, 0)
-    down_late.wait_recv()
-    finish(1, 1)
+            remote(
+                done_ref.at[span], out_ref.at[span], out_sem.at[0, half], out_sem.at[1, half], owner
+            ).start()
+
+    arrived(3)
+    arrived(4)
+    finish(0, 3, 4)
+    arrived(2)
+    arrived(5)
+    finish(1, 2, 5)
     for half in range(2):
-        span = pl.ds(half * 8, 8)
-        copy = remote(done.at[span], out_ref.at[span], out_sem.at[0, half], out_sem.at[1, half], owner)
+        span = pl.ds(half * HALF, HALF)
+        copy = remote(done_ref.at[span], out_ref.at[span], out_sem.at[0, half], out_sem.at[1, half], owner)
         copy.wait_recv()
 
         @pl.when(jnp.logical_not(same))
@@ -412,17 +471,19 @@
         reduce_kernel,
         out_shape=jax.ShapeDtypeStruct((16, BS, BS), jnp.bfloat16),
         in_specs=[ANY],
-        out_specs=ANY,
+        out_specs=pl.BlockSpec(memory_space=pltpu.VMEM),
         scratch_shapes=[
             pltpu.VMEM((4, 16, BS, BS), f32),
             pltpu.VMEM((4, 16, BS, BS), f32),
-            pltpu.VMEM((2, 8, BS, BS), f32),
-            pltpu.VMEM((2, 16, BS, BS), f32),
             pltpu.VMEM((16, BS, BS), jnp.bfloat16),
-            dma((4,)), dma((2, 4)), dma((2, 2)), dma((2, 4)), dma((2, 2)),
+            pltpu.VMEM((6, HALF, BS, BS), jnp.int16),
+            pltpu.VMEM((6, HALF, BS), f32),
+            pltpu.VMEM((6, HALF, BS, BS), jnp.int16),
+            pltpu.VMEM((6, HALF, BS), f32),
+            dma((4,)), dma((2, 4)), dma((6,)), dma((6,)), dma((6,)), dma((6,)), dma((2, 2)),
         ],
         compiler_params=pltpu.CompilerParams(
-            collective_id=1, has_side_effects=True, vmem_limit_bytes=40 * 2**20
+            collective_id=1, has_side_effects=True, vmem_limit_bytes=60 * 2**20
         ),
         name="reduce_sums",
     )(part)
@@ -432,7 +493,6 @@
     x_hi, x_lo, core, y, z = place()
     layer = y * 2 + core
     rows = lax.dynamic_slice(a_rows, (layer * 4, 0, x_hi * 2 + x_lo, 0), (4, 4, 1, 16)).reshape(16, 16)
-    rows = jnp.concatenate([rows, jnp.sum(rows >= 0, axis=1, keepdims=True, dtype=jnp.int32)], axis=1)
     cols = lax.dynamic_slice(b_cols, (layer * 4, 0, z, 0), (4, 4, 1, 8)).reshape(16, 8)
     panel_a, panel_b, twin_pos = gather_panels(a_blocks[:, 0, 0], b_blocks[:, 0, 0, 0], c_pos)
     part = partial_sums(

time: 163 us -> 133 us (0.82)
  the two profiles are of different devices: /device:TPU:57 before, /device:TPU:1 now
where the time goes in v1:
time: 133 us; the launch traced here: 132 us
  Pallas kernels  128 us (96%)
  local copies, waits for them, and re-layouts  4.18 us (3%)
    pallas_call x1, Pallas kernels, gather_panels(): pl.pallas_call(gather_kernel, out_shape=(jax.ShapeDtypeStruct((4, 8, 4, 2...  84.2 us
    pallas_call x1, Pallas kernels, reduce_sums(): pl.pallas_call(reduce_kernel, out_shape=jax.ShapeDtypeStruct((16, BS, BS)...  32.3 us
    pallas_call x1, Pallas kernels, partial_sums(): pl.pallas_call(product_kernel, out_shape=jax.ShapeDtypeStruct((BS, BS, BS...  11.1 us

profile of v1, /device:TPU:1, one launch (start us, length us, event | category | flops | bytes accessed | tf_op | source)
XLA Modules:
  0.0 131.7 jit_solution(14304084781565351778)
XLA Ops:
  0.0 0.0 copy-start
  0.0 0.8 constant_dynamic-slice_fusion
  0.8 0.7 copy.7
  1.5 0.0 copy-done
  1.5 0.1 constant_dynamic-slice_fusion.1
  1.6 0.7 copy.6
  2.3 84.2 %gather_panels.1 = (bf16[4,8,4,2,128,128]{5,4,3,2,1,0:T(8,128)(2,1)}, bf16[4,8,4,128,128]{4,3,2,1,0:T(8,128)(2,1)}, s32[1,1,128]{2,1,0:T(1,128)}) custom-call(bf16[32,2,128,128]{3,2,1,0:T(8,128)(2,1)} %bitcast.12, bf16[32,128,128]{2,1,0:T(8,128)(2,1)} %bitcast.13, s32[1,1,128]{2,1,0:T(1,128)} %mine_ref.1), custom_call_target="tpu_custom_call" | custom-call | tf_op jit(solution)/shard_map/gather_panels/pallas_call | solution.py:177
  86.5 11.1 %partial_sums.1 = f32[128,128,128]{2,1,0:T(8,128)} custom-call(s32[16,16]{1,0:T(8,128)} %bitcast.15, s32[16,8]{1,0:T(8,128)} %bitcast.14, s32[1,1,128]{2,1,0:T(1,128)} %mine_ref.1, s32[1,1,128]{2,1,0:T(1,128)} %get-tuple-element.8.twin_ref, bf16[256,128,128]{2,1,0:T(8,128)(2,1)} %bitcast.9, bf16[128,128,128]{2,1,0:T(8,128)(2,1)} %bitcast.10), custom_call_target="tpu_custom_call" | custom-call | tf_op jit(solution)/shard_map/partial_sums/pallas_call | solution.py:314
  97.6 32.3 %reduce_sums.1 = bf16[16,128,128]{2,1,0:T(8,128)(2,1)} custom-call(f32[4,2,16,128,128]{4,3,2,1,0:T(8,128)} %bitcast.8), custom_call_target="tpu_custom_call" | custom-call | tf_op jit(solution)/shard_map/reduce_sums/pallas_call | solution.py:470
  129.9 1.9 %copy.9 = bf16[1,1,16,128,128]{4,3,2,1,0:T(8,128)(2,1)} copy(bf16[1,1,16,128,128]{4,3,2,1,0:T(8,128)(2,1)} %bitcast.11) | data formatting | bytes 1048576
Async XLA Ops:
  0.0 1.5 %copy-start = (s32[32,4,4,16]{0,3,2,1:T(8,128)S(1)}, s32[32,4,4,16]{0,3,2,1:T(8,128)}, u32[]{:S(2)}) copy-start(s32[32,4,4,16]{0,3,2,1:T(8,128)} %param.6) | copy-start | bytes 98308
